TPU v7x, 128 devices: a whole 4x4x4 slice. The times are simulated.
128 devices in a mesh: ha: 8 (over z, core), wa: 16 (over y, x).
Axes of the slice: x: 4, y: 4, z: 4, core: 2. Of those that a mesh axis runs over, the one named last changes fastest.
Arguments:
- frames_in: bfloat16 [1, 240, 640, 128], P(None, 'ha', 'wa'), may hold values from -6 to 6
- cache_in: bfloat16 [2, 240, 640, 128], P(None, 'ha', 'wa'), may hold values from -6 to 6
- cache_mid: bfloat16 [2, 240, 640, 128], P(None, 'ha', 'wa'), may hold values from -6 to 6
- w_first: bfloat16 [3, 3, 3, 128, 128], replicated, may hold values from -0.109375 to 0.109375
- w_second: bfloat16 [3, 3, 3, 128, 128], replicated, may hold values from -0.109375 to 0.109375
- scale_first: float32 [1, 128], replicated, may hold values from -0.5 to 0.5
- shift_first: float32 [1, 128], replicated, may hold values from -3 to 3
- scale_second: float32 [1, 128], replicated, may hold values from -0.5 to 0.5
- shift_second: float32 [1, 128], replicated, may hold values from -3 to 3
- cotangent: bfloat16 [1, 240, 640, 128], P(None, 'ha', 'wa'), may hold values from -6 to 6
Outputs:
- grad_input: bfloat16 [1, 240, 640, 128], P(None, 'ha', 'wa')
- grad_first: float32 [3, 3, 3, 128, 128], replicated
- grad_second: float32 [3, 3, 3, 128, 128], replicated
All inputs are finite; a program needn't handle non-finite values.
Results may differ from a plain program's by a relative error of at most 0.0058.
Values may be sent and summed in bfloat16 or wider, within the bound.
No kernel may reach another device: no remote copies, remote signals or barrier semaphores. Data moves between devices by JAX's collectives and lax.ppermute only.
A program may use at most 128 MiB of HBM per device.

v0:
```python
import jax
import jax.numpy as jnp
from jax import lax
from jax.experimental import pallas as pl
from jax.experimental.pallas import tpu as pltpu
from jax.sharding import PartitionSpec as P

BF = jnp.bfloat16
F32 = jnp.float32
RIM = 4
BOTH = ("ha", "wa")


def shift(axis, step):
    count = lax.axis_size(axis)
    return [(i, i + step) for i in range(count) if 0 <= i + step < count]


def slope(value):
    sig = jax.nn.sigmoid(value)
    return sig * (1.0 + value * (1.0 - sig))


def chain_kernel(
    rows, cols, wide, low, high, w_one, w_two, sc_one, sh_one, sc_two, sh_two,
    gin, grads, field, wv_one, wv_two, slope_one, a_one, d_two, d_one, moved, sems,
):
    full, lanes = cols + 2 * RIM, field.shape[-1]
    tall = rows + 2 * RIM
    copies = [
        pltpu.make_async_copy(wide, field.at[:, RIM : RIM + rows], sems.at[0]),
        pltpu.make_async_copy(low, field.at[:, 0:RIM], sems.at[1]),
        pltpu.make_async_copy(high, field.at[:, RIM + rows : tall], sems.at[2]),
        pltpu.make_async_copy(w_one, wv_one, sems.at[3]),
        pltpu.make_async_copy(w_two, wv_two, sems.at[4]),
    ]
    for copy in copies:
        copy.start()
    for copy in copies[:4]:
        copy.wait()

    ha, wa = lax.axis_index("ha"), lax.axis_index("wa")
    image_rows, image_cols = rows * lax.axis_size("ha"), cols * lax.axis_size("wa")
    col = lax.broadcasted_iota(jnp.int32, (1, full, lanes), 1)
    own_col = col < cols
    place = jnp.where(col < cols + RIM, col, col - full) + wa * cols
    col_in = (place >= 0) & (place < image_cols)

    def in_image(start, count):
        row = lax.broadcasted_iota(jnp.int32, (count, full, lanes), 0) + (start - RIM) + ha * rows
        return (row >= 0) & (row < image_rows) & col_in

    def roll(value, step):
        return pltpu.roll(value, step % full, 1)

    def forward(piece, weight, start, count):
        lhs = jnp.concatenate(
            [piece(a, start - 1 + b, count) for a in range(3) for b in range(3)], axis=1
        )
        rhs = jnp.concatenate(
            [
                jnp.concatenate([weight[a, b, c] for c in range(3)], axis=1)
                for a in range(3)
                for b in range(3)
            ],
            axis=0,
        )
        out = jnp.dot(lhs, rhs, preferred_element_type=F32).reshape(count, full, 3 * lanes)
        return (
            roll(out[..., :lanes], 1)
            + out[..., lanes : 2 * lanes]
            + roll(out[..., 2 * lanes :], -1)
        )

    def backward(piece, weight, start, count):
        lhs = jnp.concatenate([piece(start + 1 - b, count) for b in range(3)], axis=1)
        rhs = jnp.concatenate(
            [jnp.concatenate([weight[2, b, c] for b in range(3)], axis=1) for c in range(3)],
            axis=0,
        )
        out = lax.dot_general(
            lhs, rhs, (((1,), (1,)), ((), ())), preferred_element_type=F32
        ).reshape(count, full, 3 * lanes)
        return (
            roll(out[..., :lanes], -1)
            + out[..., lanes : 2 * lanes]
            + roll(out[..., 2 * lanes :], 1)
        )

    def flat(value):
        return value.reshape(-1, lanes)

    def gradient(which, source):
        lhs = jnp.concatenate([source(a) for a in range(3)], axis=1)
        for b in range(3):
            rhs = moved[2 - b : 2 - b + rows + 2].reshape(-1, 3 * lanes)
            out = lax.dot_general(
                lhs, rhs, (((0,), (0,)), ((), ())), preferred_element_type=F32
            )
            for a in range(3):
                for c in range(3):
                    at = (((which * 3 + a) * 3 + b) * 3 + c) * lanes
                    grads[at : at + lanes, :] = out[
                        a * lanes : (a + 1) * lanes, c * lanes : (c + 1) * lanes
                    ].astype(BF)

    def spread(value, start, count):
        kept = jnp.where(own_col, value, 0.0)
        at = start - 2
        moved[at : at + count, :, :lanes] = roll(kept, -1).astype(BF)
        moved[at : at + count, :, lanes : 2 * lanes] = kept.astype(BF)
        moved[at : at + count, :, 2 * lanes :] = roll(kept, 1).astype(BF)

    zero_rows = jnp.zeros((2, full, 3 * lanes), BF)
    moved[0:2] = zero_rows
    moved[rows + 2 : rows + 4] = zero_rows

    gain_one = (1.0 + sc_one[...]).reshape(1, 1, lanes)
    gain_two = (1.0 + sc_two[...]).reshape(1, 1, lanes)
    bias_one = sh_one[...].reshape(1, 1, lanes)
    bias_two = sh_two[...].reshape(1, 1, lanes)
    step = (tall - 2) // 3
    for start in range(1, tall - 1, step):
        count = min(step, tall - 1 - start)
        m_one = (
            forward(lambda a, r, n: flat(field[a, r : r + n]), wv_one, start, count) * gain_one
            + bias_one
        )
        sig = jax.nn.sigmoid(m_one)
        inside = in_image(start, count)
        a_one[start : start + count] = jnp.where(inside, m_one * sig, 0.0).astype(BF)
        slope_one[start : start + count] = jnp.where(
            inside, sig * (1.0 + m_one * (1.0 - sig)) * gain_one, 0.0
        )

    copies[4].wait()

    def mid(a, r, n):
        return flat(a_one[r : r + n] if a == 2 else field[3 + a, r : r + n])

    step = (tall - 4) // 2
    for start in range(2, tall - 2, step):
        count = min(step, tall - 2 - start)
        m_two = forward(mid, wv_two, start, count) * gain_two + bias_two
        value = field[5, start : start + count].astype(F32) * slope(m_two) * gain_two
        d_two[start : start + count] = value.astype(BF)
        low_at, high_at = max(start, RIM), min(start + count, RIM + rows)
        spread(value[low_at - start : high_at - start], low_at, high_at - low_at)

    gradient(1, lambda a: mid(a, 3, rows + 2))

    step = (tall - 6) // 2
    for start in range(3, tall - 3, step):
        count = min(step, tall - 3 - start)
        value = (
            backward(lambda r, n: flat(d_two[r : r + n]), wv_two, start, count)
            * slope_one[start : start + count]
        )
        d_one[start : start + count] = value.astype(BF)
        low_at, high_at = max(start, RIM), min(start + count, RIM + rows)
        spread(value[low_at - start : high_at - start], low_at, high_at - low_at)

    gradient(0, lambda a: flat(field[a, 3 : 3 + rows + 2]))

    step = rows // 2
    for start in range(RIM, RIM + rows, step):
        count = min(step, RIM + rows - start)
        value = backward(lambda r, n: flat(d_one[r : r + n]), wv_one, start, count)
        gin[0, start - RIM : start - RIM + count] = value[:, :cols].astype(BF)

    used = 54 * lanes
    if grads.shape[0] > used:
        grads[used:, :] = jnp.zeros((grads.shape[0] - used, lanes), BF)


def per_device(
    frames_in, cache_in, cache_mid, w_first, w_second,
    scale_first, shift_first, scale_second, shift_second, cotangent,
):
    _, rows, cols, chans = frames_in.shape
    devices = lax.axis_size("ha") * lax.axis_size("wa")
    factor = 1.0 / (rows * cols * devices) ** 0.5
    own = jnp.concatenate([cache_in, frames_in, cache_mid, cotangent], axis=0)
    from_left = lax.ppermute(own[:, :, cols - RIM :], "wa", shift("wa", 1))
    from_right = lax.ppermute(own[:, :, :RIM], "wa", shift("wa", -1))
    wide = jnp.concatenate([own, from_right, from_left], axis=2)
    low = lax.ppermute(wide[:, rows - RIM :], "ha", shift("ha", 1))
    high = lax.ppermute(wide[:, :RIM], "ha", shift("ha", -1))

    full, tall = cols + 2 * RIM, rows + 2 * RIM
    total = 2 * 27 * chans
    share = -(-total // (8 * devices)) * 8
    anywhere = pl.BlockSpec(memory_space=pl.ANY)
    inner = pl.BlockSpec(memory_space=pltpu.VMEM)

    def body(*refs):
        chain_kernel(rows, cols, *refs)

    grad_input, grads = pl.pallas_call(
        body,
        out_shape=(
            jax.ShapeDtypeStruct((1, rows, cols, chans), BF),
            jax.ShapeDtypeStruct((share * devices, chans), BF),
        ),
        in_specs=[anywhere] * 5 + [inner] * 4,
        out_specs=(inner, inner),
        scratch_shapes=[
            pltpu.VMEM((6, tall, full, chans), BF),
            pltpu.VMEM((3, 3, 3, chans, chans), BF),
            pltpu.VMEM((3, 3, 3, chans, chans), BF),
            pltpu.VMEM((tall, full, chans), F32),
            pltpu.VMEM((tall, full, chans), BF),
            pltpu.VMEM((tall, full, chans), BF),
            pltpu.VMEM((tall, full, chans), BF),
            pltpu.VMEM((rows + 4, full, 3 * chans), BF),
            pltpu.SemaphoreType.DMA((5,)),
        ],
        compiler_params=pltpu.CompilerParams(vmem_limit_bytes=56 * 1024 * 1024),
        name="chain",
    )(wide, low, high, w_first, w_second, scale_first, shift_first, scale_second, shift_second)

    parts = lax.all_to_all(grads.reshape(devices, share, chans), BOTH, 0, 0, tiled=True)
    mine = (jnp.sum(parts.astype(F32), axis=0) * factor).astype(BF)
    every = lax.all_to_all(
        jnp.broadcast_to(mine[None], (devices, share, chans)), BOTH, 0, 0, tiled=True
    )
    every = every.reshape(share * devices, chans)
    half = total // 2
    shape = (3, 3, 3, chans, chans)
    grad_first = every[:half].astype(F32).reshape(shape)
    grad_second = every[half:total].astype(F32).reshape(shape)
    return (grad_input, grad_first, grad_second)


def solution(mesh):
    tiled = P(None, "ha", "wa", None)
    return jax.shard_map(
        per_device,
        mesh=mesh,
        in_specs=(tiled, tiled, tiled, P(), P(), P(), P(), P(), P(), tiled),
        out_specs=(tiled, P(), P()),
        check_vma=False,
    )
```

profile of v0, /device:TPU:1, one launch (start us, length us, event | category | flops | bytes accessed | tf_op | source)
XLA Modules:
  0.0 114.0 jit_solution(13146927000099000457)
XLA Ops:
  0.6 0.0 copy-start.1
  0.6 0.0 copy-start.2
  0.7 1.2 %constant_dynamic-update-slice_fusion.3 = bf16[6,30,40,128]{3,2,1,0:T(8,128)(2,1)S(1)} fusion(bf16[2,30,40,128]{3,2,1,0:T(8,128)(2,1)} %param.11), kind=kLoop, calls=%fused_computation.6 | loop fusion | bytes 1228800
  1.9 1.0 constant_dynamic-update-slice_fusion.2
  2.9 0.0 copy-done.1
  2.9 0.1 constant_dynamic-update-slice_fusion.1
  3.0 0.0 copy-done.2
  3.1 0.1 fusion.1
  3.2 1.3 %collective-permute-start = (bf16[6,30,4,128]{3,2,1,0:T(4,128)(2,1)S(1)}, bf16[6,30,4,128]{3,2,1,0:T(4,128)(2,1)S(1)}, u32[]{:S(2)}, u32[]{:S(2)}) collective-permute-start(bf16[6,30,4,128]{3,2,1,0:T(4,128)(2,1)S(1)} %get-tuple-element.9), channel_id=1, source_target_pairs={{1,0},{2,1},{3,2},{4,3},{5,4},{6,5},{7,6},{8,7},{9,8},{10,9},{11,1... | collective-permute-start | bytes 552968 | tf_op jit(solution)/shard_map/ppermute | solution.py:185
  4.5 4.6 %collective-permute-start.1 = (bf16[6,30,4,128]{3,2,1,0:T(4,128)(2,1)S(1)}, bf16[6,30,4,128]{3,2,1,0:T(4,128)(2,1)S(1)}, u32[]{:S(2)}, u32[]{:S(2)}) collective-permute-start(bf16[6,30,4,128]{3,2,1,0:T(4,128)(2,1)S(1)} %get-tuple-element.10), channel_id=1, source_target_pairs={{0,1},{1,2},{2,3},{3,4},{4,5},{5,6},{6,7},{7,8},{8,9},{9,10},{10,1... | collective-permute-start | bytes 552968 | tf_op jit(solution)/shard_map/ppermute | solution.py:184
  9.1 1.9 %collective-permute-done = bf16[6,30,4,128]{3,2,1,0:T(4,128)(2,1)S(1)} collective-permute-done((bf16[6,30,4,128]{3,2,1,0:T(4,128)(2,1)S(1)}, bf16[6,30,4,128]{3,2,1,0:T(4,128)(2,1)S(1)}, u32[]{:S(2)}, u32[]{:S(2)}) %collective-permute-start) | collective-permute-done | bytes 184352 | tf_op jit(solution)/shard_map/ppermute | solution.py:185
  11.0 0.9 collective-permute-done.1
  11.9 0.6 pad_maximum_fusion.refs_0_
  12.5 0.0 copy-start
  12.5 0.1 fusion
  12.6 3.9 %collective-permute-start.3 = (bf16[6,4,48,128]{3,2,1,0:T(8,128)(2,1)S(1)}, bf16[6,4,48,128]{3,2,1,0:T(8,128)(2,1)S(1)}, u32[]{:S(2)}, u32[]{:S(2)}) collective-permute-start(bf16[6,4,48,128]{3,2,1,0:T(8,128)(2,1)S(1)} %get-tuple-element.7), channel_id=1, source_target_pairs={{16,0},{32,16},{48,32},{64,48},{80,64},{96,80},{112,96},{17,1},{33... | collective-permute-start | bytes 884744 | tf_op jit(solution)/shard_map/ppermute | solution.py:188
  16.5 3.7 %collective-permute-start.2 = (bf16[6,4,48,128]{3,2,1,0:T(8,128)(2,1)S(1)}, bf16[6,4,48,128]{3,2,1,0:T(8,128)(2,1)S(1)}, u32[]{:S(2)}, u32[]{:S(2)}) collective-permute-start(bf16[6,4,48,128]{3,2,1,0:T(8,128)(2,1)S(1)} %get-tuple-element.8), channel_id=1, source_target_pairs={{0,16},{16,32},{32,48},{48,64},{64,80},{80,96},{96,112},{1,17},{17... | collective-permute-start | bytes 884744 | tf_op jit(solution)/shard_map/ppermute | solution.py:187
  20.2 2.5 %collective-permute-done.3.refs_2_ = bf16[6,4,48,128]{3,2,1,0:T(8,128)(2,1)S(1)} collective-permute-done((bf16[6,4,48,128]{3,2,1,0:T(8,128)(2,1)S(1)}, bf16[6,4,48,128]{3,2,1,0:T(8,128)(2,1)S(1)}, u32[]{:S(2)}, u32[]{:S(2)}) %collective-permute-start.3) | collective-permute-done | bytes 294944 | tf_op jit(solution)/shard_map/ppermute | solution.py:188
  22.7 0.0 copy-start.3
  22.7 1.2 %collective-permute-done.2.refs_1_ = bf16[6,4,48,128]{3,2,1,0:T(8,128)(2,1)S(1)} collective-permute-done((bf16[6,4,48,128]{3,2,1,0:T(8,128)(2,1)S(1)}, bf16[6,4,48,128]{3,2,1,0:T(8,128)(2,1)S(1)}, u32[]{:S(2)}, u32[]{:S(2)}) %collective-permute-start.2) | collective-permute-done | bytes 294944 | tf_op jit(solution)/shard_map/ppermute | solution.py:187
  23.8 0.0 copy-done
  23.9 0.0 copy-done.3
  23.9 0.0 copy-start.4
  23.9 0.7 copy-done.4
  24.6 13.7 %chain.1 = (bf16[1,30,40,128]{3,2,1,0:T(8,128)(2,1)}, bf16[7168,128]{1,0:T(8,128)(2,1)}) custom-call(bf16[6,30,48,128]{3,2,1,0:T(8,128)(2,1)} %copy-done, bf16[6,4,48,128]{3,2,1,0:T(8,128)(2,1)} %copy-done.4, bf16[6,4,48,128]{3,2,1,0:T(8,128)(2,1)} %copy-done.3, bf16[3,3,3,128,128]{4,3,2,1,0:T(8,128)(2,1)} %refs_3_.1, bf16[3,3,3,128,128]{4,3,2,1,0:T(8,128)(2,1)} %refs_4_.1, ...), custom_call_target="tpu_custom_call" | custom-call | tf_op jit(solution)/shard_map/chain/pallas_call | solution.py:199
  38.3 40.7 %all_to_all.10 = bf16[128,56,128]{2,1,0:T(8,128)(2,1)S(1)} all-to-all(bf16[128,56,128]{2,1,0:T(8,128)(2,1)} %bitcast.9), channel_id=1, replica_groups=mesh['ha'=8,'wa'=16] {'ha','wa'}, dimensions={0} | all-to-all | bytes 3670016 | tf_op jit(solution)/shard_map/all_to_all | solution.py:222
  79.0 0.3 convert_reduce_fusion
  79.3 0.2 broadcast_in_dim.2
  79.6 31.5 %all_to_all.11 = bf16[128,56,128]{2,1,0:T(8,128)(2,1)S(1)} all-to-all(bf16[128,56,128]{2,1,0:T(8,128)(2,1)S(1)} %broadcast_in_dim.2), channel_id=1, replica_groups=mesh['ha'=8,'wa'=16] {'ha','wa'}, dimensions={0} | all-to-all | bytes 3670016 | tf_op jit(solution)/shard_map/all_to_all | solution.py:224
  111.0 0.1 fusion.2
  111.2 1.4 %convert.2 = f32[3,3,3,128,128]{4,3,2,1,0:T(8,128)} convert(bf16[3,3,3,128,128]{4,3,2,1,0:T(8,128)(2,1)S(1)} %bitcast.8) | non-fusion elementwise | flops 442368 | bytes 2654208 | tf_op jit(solution)/shard_map/reshape | solution.py:230
  112.6 1.4 %convert.3 = f32[3,3,3,128,128]{4,3,2,1,0:T(8,128)} convert(bf16[3,3,3,128,128]{4,3,2,1,0:T(8,128)(2,1)S(1)} %bitcast.7) | non-fusion elementwise | flops 442368 | bytes 2654208 | tf_op jit(solution)/shard_map/reshape | solution.py:231
  (2 shorter events, 0.1 us)
Async XLA Ops:
  0.6 2.2 %copy-start.1 = (bf16[2,30,40,128]{3,2,1,0:T(8,128)(2,1)S(1)}, bf16[2,30,40,128]{3,2,1,0:T(8,128)(2,1)}, u32[]{:S(2)}) copy-start(bf16[2,30,40,128]{3,2,1,0:T(8,128)(2,1)} %param.12) | copy-start | bytes 1843204
  0.6 2.4 %copy-start.2 = (bf16[1,30,40,128]{3,2,1,0:T(8,128)(2,1)S(1)}, bf16[1,30,40,128]{3,2,1,0:T(8,128)(2,1)}, u32[]{:S(2)}) copy-start(bf16[1,30,40,128]{3,2,1,0:T(8,128)(2,1)} %param.19) | copy-start | bytes 921604
  3.2 7.8 %collective-permute-start = (bf16[6,30,4,128]{3,2,1,0:T(4,128)(2,1)S(1)}, bf16[6,30,4,128]{3,2,1,0:T(4,128)(2,1)S(1)}, u32[]{:S(2)}, u32[]{:S(2)}) collective-permute-start(bf16[6,30,4,128]{3,2,1,0:T(4,128)(2,1)S(1)} %get-tuple-element.9), channel_id=1, source_target_pairs={{1,0},{2,1},{3,2},{4,3},{5,4},{6,5},{7,6},{8,7},{9,8},{10,9},{11,1... | collective-permute-start | bytes 552968 | tf_op jit(solution)/shard_map/ppermute | solution.py:185
  4.5 7.4 %collective-permute-start.1 = (bf16[6,30,4,128]{3,2,1,0:T(4,128)(2,1)S(1)}, bf16[6,30,4,128]{3,2,1,0:T(4,128)(2,1)S(1)}, u32[]{:S(2)}, u32[]{:S(2)}) collective-permute-start(bf16[6,30,4,128]{3,2,1,0:T(4,128)(2,1)S(1)} %get-tuple-element.10), channel_id=1, source_target_pairs={{0,1},{1,2},{2,3},{3,4},{4,5},{5,6},{6,7},{7,8},{8,9},{9,10},{10,1... | collective-permute-start | bytes 552968 | tf_op jit(solution)/shard_map/ppermute | solution.py:184
  12.5 11.4 %copy-start = (bf16[6,30,48,128]{3,2,1,0:T(8,128)(2,1)}, bf16[6,30,48,128]{3,2,1,0:T(8,128)(2,1)S(1)}, u32[]{:S(2)}) copy-start(bf16[6,30,48,128]{3,2,1,0:T(8,128)(2,1)S(1)} %pad_maximum_fusion.refs_0_) | copy-start | bytes 6635524
  12.6 10.1 %collective-permute-start.3 = (bf16[6,4,48,128]{3,2,1,0:T(8,128)(2,1)S(1)}, bf16[6,4,48,128]{3,2,1,0:T(8,128)(2,1)S(1)}, u32[]{:S(2)}, u32[]{:S(2)}) collective-permute-start(bf16[6,4,48,128]{3,2,1,0:T(8,128)(2,1)S(1)} %get-tuple-element.7), channel_id=1, source_target_pairs={{16,0},{32,16},{48,32},{64,48},{80,64},{96,80},{112,96},{17,1},{33... | collective-permute-start | bytes 884744 | tf_op jit(solution)/shard_map/ppermute | solution.py:188
  16.5 7.3 %collective-permute-start.2 = (bf16[6,4,48,128]{3,2,1,0:T(8,128)(2,1)S(1)}, bf16[6,4,48,128]{3,2,1,0:T(8,128)(2,1)S(1)}, u32[]{:S(2)}, u32[]{:S(2)}) collective-permute-start(bf16[6,4,48,128]{3,2,1,0:T(8,128)(2,1)S(1)} %get-tuple-element.8), channel_id=1, source_target_pairs={{0,16},{16,32},{32,48},{48,64},{64,80},{80,96},{96,112},{1,17},{17... | collective-permute-start | bytes 884744 | tf_op jit(solution)/shard_map/ppermute | solution.py:187
  22.7 1.2 %copy-start.3 = (bf16[6,4,48,128]{3,2,1,0:T(8,128)(2,1)}, bf16[6,4,48,128]{3,2,1,0:T(8,128)(2,1)S(1)}, u32[]{:S(2)}) copy-start(bf16[6,4,48,128]{3,2,1,0:T(8,128)(2,1)S(1)} %collective-permute-done.3.refs_2_) | copy-start | bytes 884740
  23.9 0.7 copy-start.4
where the time goes:
time: 114 us
  blocking collectives  72.2 us (63%)
  Pallas kernels  13.7 us (12%)
  starting transfers between devices  13.5 us (12%)
  waiting for transfers between devices  6.43 us (6%)
  other arithmetic  3.72 us (3%)
  local copies, waits for them, and re-layouts  3.65 us (3%)
    all_to_all x1, blocking collectives, per_device(): lax.all_to_all(grads.reshape(devices, share, chans), BOTH, 0, 0, tiled=True)  40.7 us
    all_to_all x1, blocking collectives, per_device(): lax.all_to_all(jnp.broadcast_to(mine[None], (devices, share, chans)), BOT...  31.5 us
    pallas_call x1, Pallas kernels, per_device(): pl.pallas_call(body, out_shape=(jax.ShapeDtypeStruct((1, rows, cols, chan...  13.7 us
    ppermute x1, starting transfers between devices, per_device(): from_left = lax.ppermute(own[:, :, cols - RIM:], 'wa', shift('wa', 1))  4.58 us
    ppermute x1, starting transfers between devices, per_device(): high = lax.ppermute(wide[:, :RIM], 'ha', shift('ha', -1))  3.95 us
    ppermute x1, starting transfers between devices, per_device(): low = lax.ppermute(wide[:, rows - RIM:], 'ha', shift('ha', 1))  3.69 us
    unnamed x13, local copies, waits for them, and re-layouts  3.05 us
    ppermute x1, waiting for transfers between devices, per_device(): high = lax.ppermute(wide[:, :RIM], 'ha', shift('ha', -1))  2.46 us
  transfers between devices with their start and end apart: 4, of which 4 were waited for; matrix products, arithmetic and copies ran while one was open for 0% of the time, Pallas kernels for 0%

commit v1 on v0

--- a/solution.py
+++ b/solution.py
@@ -11,9 +11,19 @@
 BOTH = ("ha", "wa")
 
 
-def shift(axis, step):
+def swaps(axis):
     count = lax.axis_size(axis)
-    return [(i, i + step) for i in range(count) if 0 <= i + step < count]
+    first = [(i, i ^ 1) for i in range(count)]
+    second = [(i, i + 1 if i % 2 else i - 1) for i in range(1, count - 1)]
+    return first, second
+
+
+def trade(axis, head, tail):
+    odd = lax.axis_index(axis) % 2 == 1
+    first, second = swaps(axis)
+    near = lax.ppermute(jnp.where(odd, head, tail), axis, first)
+    far = lax.ppermute(jnp.where(odd, tail, head), axis, second)
+    return near, far
 
 
 def slope(value):
@@ -22,24 +32,53 @@
 
 
 def chain_kernel(
-    rows, cols, wide, low, high, w_one, w_two, sc_one, sh_one, sc_two, sh_two,
-    gin, grads, field, wv_one, wv_two, slope_one, a_one, d_two, d_one, moved, sems,
+    rows, cols, cache_in, frames_in, cache_mid, cot, row_near, row_far, col_near, col_far,
+    w_one, w_two, sc_one, sh_one, sc_two, sh_two,
+    gin, keep, send, field, slope_one, a_one, d_two, d_one, moved, grads, sems,
 ):
     full, lanes = cols + 2 * RIM, field.shape[-1]
     tall = rows + 2 * RIM
-    copies = [
-        pltpu.make_async_copy(wide, field.at[:, RIM : RIM + rows], sems.at[0]),
-        pltpu.make_async_copy(low, field.at[:, 0:RIM], sems.at[1]),
-        pltpu.make_async_copy(high, field.at[:, RIM + rows : tall], sems.at[2]),
-        pltpu.make_async_copy(w_one, wv_one, sems.at[3]),
-        pltpu.make_async_copy(w_two, wv_two, sems.at[4]),
-    ]
-    for copy in copies:
-        copy.start()
-    for copy in copies[:4]:
-        copy.wait()
-
     ha, wa = lax.axis_index("ha"), lax.axis_index("wa")
+    odd_row, odd_col = ha % 2 == 1, wa % 2 == 1
+    core = ha % 2
+
+    def pick(odd, one, other):
+        return jnp.where(odd, one.astype(F32), other.astype(F32))
+
+    def assemble(frame, top, block, at):
+        count, high = block.shape[:2]
+        size = count * high * RIM
+        near, far = col_near[at : at + size], col_far[at : at + size]
+        left = pick(odd_col, near, far).reshape(-1, 2 * RIM, lanes)
+        right = pick(odd_col, far, near).reshape(-1, 2 * RIM, lanes)
+        lower = lax.broadcasted_iota(jnp.int32, left.shape, 1) < RIM
+        rim = jnp.stack(
+            [
+                jnp.where(lower, right, pltpu.roll(left, RIM, 1)),
+                jnp.where(lower, pltpu.roll(right, RIM, 1), left),
+            ],
+            axis=1,
+        ).reshape(count, high, 2 * RIM, lanes)
+        field[frame : frame + count, top : top + high] = jnp.concatenate(
+            [block, rim], axis=2
+        ).astype(BF)
+
+    own_strip, corner = rows * RIM, RIM * RIM
+    for frame, source in ((0, cache_in), (2, frames_in), (3, cache_mid), (5, cot)):
+        assemble(frame, RIM, source[...].astype(F32), frame * own_strip)
+    near_at, far_at = 6 * own_strip, 6 * (own_strip + corner)
+    near_block, far_block = row_near[...].astype(F32), row_far[...].astype(F32)
+
+    @pl.when(odd_row)
+    def _():
+        assemble(0, 0, near_block, near_at)
+        assemble(0, RIM + rows, far_block, far_at)
+
+    @pl.when(jnp.logical_not(odd_row))
+    def _():
+        assemble(0, 0, far_block, far_at)
+        assemble(0, RIM + rows, near_block, near_at)
+
     image_rows, image_cols = rows * lax.axis_size("ha"), cols * lax.axis_size("wa")
     col = lax.broadcasted_iota(jnp.int32, (1, full, lanes), 1)
     own_col = col < cols
@@ -99,8 +138,8 @@
             )
             for a in range(3):
                 for c in range(3):
-                    at = (((which * 3 + a) * 3 + b) * 3 + c) * lanes
-                    grads[at : at + lanes, :] = out[
+                    at = ((a * 3 + b) * 3 + c) * lanes
+                    grads[which, at : at + lanes, :] = out[
                         a * lanes : (a + 1) * lanes, c * lanes : (c + 1) * lanes
                     ].astype(BF)
 
@@ -114,6 +153,9 @@
     zero_rows = jnp.zeros((2, full, 3 * lanes), BF)
     moved[0:2] = zero_rows
     moved[rows + 2 : rows + 4] = zero_rows
+    used = 27 * lanes
+    if grads.shape[1] > used:
+        grads[:, used:, :] = jnp.zeros((2, grads.shape[1] - used, lanes), BF)
 
     gain_one = (1.0 + sc_one[...]).reshape(1, 1, lanes)
     gain_two = (1.0 + sc_two[...]).reshape(1, 1, lanes)
@@ -123,7 +165,7 @@
     for start in range(1, tall - 1, step):
         count = min(step, tall - 1 - start)
         m_one = (
-            forward(lambda a, r, n: flat(field[a, r : r + n]), wv_one, start, count) * gain_one
+            forward(lambda a, r, n: flat(field[a, r : r + n]), w_one, start, count) * gain_one
             + bias_one
         )
         sig = jax.nn.sigmoid(m_one)
@@ -133,15 +175,13 @@
             inside, sig * (1.0 + m_one * (1.0 - sig)) * gain_one, 0.0
         )
 
-    copies[4].wait()
-
     def mid(a, r, n):
         return flat(a_one[r : r + n] if a == 2 else field[3 + a, r : r + n])
 
     step = (tall - 4) // 2
     for start in range(2, tall - 2, step):
         count = min(step, tall - 2 - start)
-        m_two = forward(mid, wv_two, start, count) * gain_two + bias_two
+        m_two = forward(mid, w_two, start, count) * gain_two + bias_two
         value = field[5, start : start + count].astype(F32) * slope(m_two) * gain_two
         d_two[start : start + count] = value.astype(BF)
         low_at, high_at = max(start, RIM), min(start + count, RIM + rows)
@@ -153,7 +193,7 @@
     for start in range(3, tall - 3, step):
         count = min(step, tall - 3 - start)
         value = (
-            backward(lambda r, n: flat(d_two[r : r + n]), wv_two, start, count)
+            backward(lambda r, n: flat(d_two[r : r + n]), w_two, start, count)
             * slope_one[start : start + count]
         )
         d_one[start : start + count] = value.astype(BF)
@@ -161,16 +201,21 @@
         spread(value[low_at - start : high_at - start], low_at, high_at - low_at)
 
     gradient(0, lambda a: flat(field[a, 3 : 3 + rows + 2]))
+    out_copies = [
+        pltpu.make_async_copy(grads.at[core], keep, sems.at[0]),
+        pltpu.make_async_copy(grads.at[1 - core], send, sems.at[1]),
+    ]
+    for copy in out_copies:
+        copy.start()
 
     step = rows // 2
     for start in range(RIM, RIM + rows, step):
         count = min(step, RIM + rows - start)
-        value = backward(lambda r, n: flat(d_one[r : r + n]), wv_one, start, count)
+        value = backward(lambda r, n: flat(d_one[r : r + n]), w_one, start, count)
         gin[0, start - RIM : start - RIM + count] = value[:, :cols].astype(BF)
 
-    used = 54 * lanes
-    if grads.shape[0] > used:
-        grads[used:, :] = jnp.zeros((grads.shape[0] - used, lanes), BF)
+    for copy in out_copies:
+        copy.wait()
 
 
 def per_device(
@@ -180,55 +225,76 @@
     _, rows, cols, chans = frames_in.shape
     devices = lax.axis_size("ha") * lax.axis_size("wa")
     factor = 1.0 / (rows * cols * devices) ** 0.5
-    own = jnp.concatenate([cache_in, frames_in, cache_mid, cotangent], axis=0)
-    from_left = lax.ppermute(own[:, :, cols - RIM :], "wa", shift("wa", 1))
-    from_right = lax.ppermute(own[:, :, :RIM], "wa", shift("wa", -1))
-    wide = jnp.concatenate([own, from_right, from_left], axis=2)
-    low = lax.ppermute(wide[:, rows - RIM :], "ha", shift("ha", 1))
-    high = lax.ppermute(wide[:, :RIM], "ha", shift("ha", -1))
+    fields = [cache_in, frames_in, cache_mid, cotangent]
+
+    def edges(cut):
+        return jnp.concatenate([cut(field) for field in fields], axis=0)
+
+    row_near, row_far = trade(
+        "ha", edges(lambda v: v[:, :RIM]), edges(lambda v: v[:, rows - RIM :])
+    )
+
+    def strip(cut):
+        pieces = [edges(cut), cut(row_near), cut(row_far)]
+        return jnp.concatenate([piece.reshape(-1, chans) for piece in pieces], axis=0)
+
+    col_near, col_far = trade(
+        "wa", strip(lambda v: v[:, :, :RIM]), strip(lambda v: v[:, :, cols - RIM :])
+    )
 
     full, tall = cols + 2 * RIM, rows + 2 * RIM
-    total = 2 * 27 * chans
-    share = -(-total // (8 * devices)) * 8
+    chips = devices // 2
+    total = 27 * chans
+    share = -(-total // (8 * chips)) * 8
     anywhere = pl.BlockSpec(memory_space=pl.ANY)
     inner = pl.BlockSpec(memory_space=pltpu.VMEM)
 
     def body(*refs):
         chain_kernel(rows, cols, *refs)
 
-    grad_input, grads = pl.pallas_call(
+    grad_input, keep, send = pl.pallas_call(
         body,
         out_shape=(
             jax.ShapeDtypeStruct((1, rows, cols, chans), BF),
-            jax.ShapeDtypeStruct((share * devices, chans), BF),
+            jax.ShapeDtypeStruct((share * chips, chans), BF),
+            jax.ShapeDtypeStruct((share * chips, chans), BF),
         ),
-        in_specs=[anywhere] * 5 + [inner] * 4,
-        out_specs=(inner, inner),
+        in_specs=[inner] * 14,
+        out_specs=(inner, anywhere, anywhere),
         scratch_shapes=[
             pltpu.VMEM((6, tall, full, chans), BF),
-            pltpu.VMEM((3, 3, 3, chans, chans), BF),
-            pltpu.VMEM((3, 3, 3, chans, chans), BF),
             pltpu.VMEM((tall, full, chans), F32),
             pltpu.VMEM((tall, full, chans), BF),
             pltpu.VMEM((tall, full, chans), BF),
             pltpu.VMEM((tall, full, chans), BF),
             pltpu.VMEM((rows + 4, full, 3 * chans), BF),
-            pltpu.SemaphoreType.DMA((5,)),
+            pltpu.VMEM((2, share * chips, chans), BF),
+            pltpu.SemaphoreType.DMA((2,)),
         ],
-        compiler_params=pltpu.CompilerParams(vmem_limit_bytes=56 * 1024 * 1024),
+        compiler_params=pltpu.CompilerParams(vmem_limit_bytes=40 * 1024 * 1024),
         name="chain",
-    )(wide, low, high, w_first, w_second, scale_first, shift_first, scale_second, shift_second)
-
-    parts = lax.all_to_all(grads.reshape(devices, share, chans), BOTH, 0, 0, tiled=True)
-    mine = (jnp.sum(parts.astype(F32), axis=0) * factor).astype(BF)
-    every = lax.all_to_all(
-        jnp.broadcast_to(mine[None], (devices, share, chans)), BOTH, 0, 0, tiled=True
+    )(
+        cache_in, frames_in, cache_mid, cotangent, row_near, row_far, col_near, col_far,
+        w_first, w_second, scale_first, shift_first, scale_second, shift_second,
     )
-    every = every.reshape(share * devices, chans)
-    half = total // 2
+
+    pairs, _ = swaps("ha")
+    chip_sum = (keep.astype(F32) + lax.ppermute(send, "ha", pairs).astype(F32)).astype(BF)
+    cores = [[c for c in range(devices) if (c // lax.axis_size("wa")) % 2 == k] for k in range(2)]
+
+    def spread_out(value):
+        return lax.all_to_all(
+            value.reshape(chips, share, chans), BOTH, 0, 0, axis_index_groups=cores, tiled=True
+        )
+
+    mine = (jnp.sum(spread_out(chip_sum).astype(F32), axis=0) * factor).astype(BF)
+    one = spread_out(jnp.broadcast_to(mine[None], (chips, share, chans))).reshape(-1, chans)
+    other = lax.ppermute(one, "ha", pairs)
+    even = lax.axis_index("ha") % 2 == 0
     shape = (3, 3, 3, chans, chans)
-    grad_first = every[:half].astype(F32).reshape(shape)
-    grad_second = every[half:total].astype(F32).reshape(shape)
+    one, other = one[:total].astype(F32), other[:total].astype(F32)
+    grad_first = jnp.where(even, one, other).reshape(shape)
+    grad_second = jnp.where(even, other, one).reshape(shape)
     return (grad_input, grad_first, grad_second)
 
 

time: 114 us -> 99.4 us (0.87)
  blocking collectives: 72.2 us -> 48.7 us
  waiting for transfers between devices: 6.43 us -> 11.5 us
  local copies, waits for them, and re-layouts: 3.65 us -> 6.99 us
  other arithmetic: 3.72 us -> 5.41 us
    all_to_all x2, blocking collectives: 72.2 us -> 48.7 us  [spread_out(): lax.all_to_all(value.reshape(chips, share, chans), BOTH, 0, 0, axis_index...]
    ppermute x4 -> x6, waiting for transfers between devices: 6.43 us -> 11.5 us  [the longest x2 5.03 us: trade(): near = lax.ppermute(jnp.where(odd, head, tail), axis, first)]
    select_n x0 -> x3, other arithmetic: none -> 3.97 us  [the longest x1 2.02 us: per_device(): grad_second = jnp.where(even, other, one).reshape(shape)]
    slice x3 -> x8, local copies, waits for them, and re-layouts: 0.32 us -> 3.91 us  [the longest x2 2.01 us: per_device(): v[:, :RIM]]
    reshape x2 -> x0, other arithmetic: 2.81 us -> none  [the longest x1 1.4 us: per_device(): grad_first = every[:half].astype(F32).reshape(shape)]
    ppermute x4 -> x6, starting transfers between devices: 13.5 us -> 12.7 us  [the longest x2 5.6 us: trade(): far = lax.ppermute(jnp.where(odd, tail, head), axis, second)]
    unnamed x13 -> x20, local copies, waits for them, and re-layouts: 3.05 us -> 2.96 us
  transfers between devices with their start and end apart: 4 -> 6, of which waited for: 4 -> 4; matrix products, arithmetic and copies ran while one was open for 0% -> 2% of each run, Pallas kernels for 0% -> 0%
where the time goes in v1:
time: 99.4 us; the launch traced here: 99 us
  blocking collectives  48.7 us (49%)
  Pallas kernels  12.8 us (13%)
  starting transfers between devices  12.7 us (13%)
  waiting for transfers between devices  11.5 us (12%)
  local copies, waits for them, and re-layouts  6.99 us (7%)
  other arithmetic  5.41 us (5%)
    all_to_all x2, blocking collectives, spread_out(): lax.all_to_all(value.reshape(chips, share, chans), BOTH, 0, 0, axis_index...  48.7 us
    pallas_call x1, Pallas kernels, per_device(): pl.pallas_call(body, out_shape=(jax.ShapeDtypeStruct((1, rows, cols, chan...  12.8 us
    ppermute x2, starting transfers between devices, trade(): far = lax.ppermute(jnp.where(odd, tail, head), axis, second)  5.6 us
    ppermute x2, waiting for transfers between devices, trade(): near = lax.ppermute(jnp.where(odd, head, tail), axis, first)  5.03 us
    ppermute x2, starting transfers between devices, trade(): near = lax.ppermute(jnp.where(odd, head, tail), axis, first)  3.82 us
    ppermute x1, starting transfers between devices, per_device(): other = lax.ppermute(one, 'ha', pairs)  3.19 us
    unnamed x20, local copies, waits for them, and re-layouts  2.96 us
    ppermute x1, waiting for transfers between devices, per_device(): lax.ppermute(send, 'ha', pairs).astype(F32)  2.46 us
  transfers between devices with their start and end apart: 6, of which 4 were waited for; matrix products, arithmetic and copies ran while one was open for 2% of the time, Pallas kernels for 0%

profile of v1, /device:TPU:1, one launch (start us, length us, event | category | flops | bytes accessed | tf_op | source)
XLA Modules:
  0.0 99.0 jit_solution(14586678415843722496)
XLA Ops:
  0.6 0.0 copy-start.4
  0.6 0.0 copy-start.1
  0.7 0.0 copy-start
  0.7 1.0 fusion.6
  1.6 1.0 %fusion.2 = (bf16[2,4,40,128]{3,2,1,0:T(8,128)(2,1)S(1)}, bf16[2,4,40,128]{3,2,1,0:T(8,128)(2,1)S(1)}, bf16[2,4,40,128]{3,2,1,0:T(8,128)(2,1)S(1)}, bf16[2,4,40,128]{3,2,1,0:T(8,128)(2,1)S(1)}) fusion(bf16[2,30,40,128]{3,2,1,0:T(8,128)(2,1)} %refs_0_.1, bf16[2,30,40,128]{3,2,1,0:T(8,128)(2,1)} %refs_2_.1), kind=kLoop, calls=%fused_computation.17 | loop fusion | bytes 655360 | tf_op jit(solution)/shard_map/slice | solution.py:234
  2.7 0.0 copy-start.2
  2.7 0.0 copy-start.3
  2.7 0.0 copy-start.6
  2.7 0.8 broadcast_select_fusion
  3.6 4.9 %collective-permute-start.1 = (bf16[6,4,40,128]{3,2,1,0:T(8,128)(2,1)}, bf16[6,4,40,128]{3,2,1,0:T(8,128)(2,1)S(1)}, u32[]{:S(2)}, u32[]{:S(2)}) collective-permute-start(bf16[6,4,40,128]{3,2,1,0:T(8,128)(2,1)} %get-tuple-element.19), channel_id=1, source_target_pairs={{16,32},{32,16},{48,64},{64,48},{80,96},{96,80},{17,33},{33,17},{4... | collective-permute-start | bytes 737288 | tf_op jit(solution)/shard_map/ppermute | solution.py:25
  8.5 0.1 collective-permute-start
  8.6 0.0 copy-done.4
  8.7 0.0 copy-done
  8.7 0.1 fusion
  8.7 0.0 copy-done.1
  8.7 0.1 fusion.1
  8.8 0.9 fusion.5
  9.7 1.0 %pad_maximum_fusion.4 = (bf16[6,30,4,128]{3,2,1,0:T(4,128)(2,1)}, bf16[6,30,4,128]{3,2,1,0:T(4,128)(2,1)}) fusion(bf16[1,30,4,128]{3,2,1,0:T(4,128)(2,1)S(1)} %get-tuple-element.25, bf16[2,30,4,128]{3,2,1,0:T(4,128)(2,1)S(1)} %get-tuple-element.13, bf16[1,30,4,128]{3,2,1,0:T(4,128)(2,1)S(1)} %get-tuple-element.23, ...), kind=kLoop, calls=%fused_computation.12 | loop fusion | flops 552960 | bytes 737280 | tf_op jit(solution)/shard_map/concatenate | solution.py:231
  10.7 1.9 %collective-permute-done.1.refs_5_ = bf16[6,4,40,128]{3,2,1,0:T(8,128)(2,1)S(1)} collective-permute-done((bf16[6,4,40,128]{3,2,1,0:T(8,128)(2,1)}, bf16[6,4,40,128]{3,2,1,0:T(8,128)(2,1)S(1)}, u32[]{:S(2)}, u32[]{:S(2)}) %collective-permute-start.1) | collective-permute-done | bytes 245792 | tf_op jit(solution)/shard_map/ppermute | solution.py:25
  12.6 0.0 collective-permute-done.refs_4_
  12.6 0.8 fusion.8
  13.5 1.1 %broadcast_select_fusion.2 = (bf16[912,128]{1,0:T(8,128)(2,1)S(1)}, bf16[912,128]{1,0:T(8,128)(2,1)S(1)}) fusion(pred[]{:T(512)S(6)} %eq.14, bf16[96,128]{1,0:T(8,128)(2,1)S(1)} %bitcast.18, bf16[96,128]{1,0:T(8,128)(2,1)S(1)} %bitcast.20, bf16[720,128]{1,0:T(8,128)(2,1)} %bitcast.16, bf16[96,128]{1,0:T(8,128)(2,1)S(1)} %bitcast.17, ...), kind=kLoop, calls=%fused_computation.10 | loop fusion | flops 1634304 | bytes 933889 | tf_op jit(solution)/shard_map/jit(_where)/select_n | solution.py:25
  14.6 0.7 collective-permute-start.3
  15.3 3.7 %collective-permute-start.2 = (bf16[912,128]{1,0:T(8,128)(2,1)S(1)}, bf16[912,128]{1,0:T(8,128)(2,1)S(1)}, u32[]{:S(2)}, u32[]{:S(2)}) collective-permute-start(bf16[912,128]{1,0:T(8,128)(2,1)S(1)} %get-tuple-element.22), channel_id=1, source_target_pairs={{0,1},{1,0},{2,3},{3,2},{4,5},{5,4},{6,7},{7,6},{8,9},{9,8},{10,11... | collective-permute-start | bytes 700424 | tf_op jit(solution)/shard_map/ppermute | solution.py:24
  19.0 0.0 collective-permute-done.3.refs_7_
  19.0 5.0 %collective-permute-done.2.refs_6_ = bf16[912,128]{1,0:T(8,128)(2,1)S(1)} collective-permute-done((bf16[912,128]{1,0:T(8,128)(2,1)S(1)}, bf16[912,128]{1,0:T(8,128)(2,1)S(1)}, u32[]{:S(2)}, u32[]{:S(2)}) %collective-permute-start.2) | collective-permute-done | bytes 233504 | tf_op jit(solution)/shard_map/ppermute | solution.py:24
  24.0 0.0 copy-done.2
  24.0 0.0 copy-done.3
  24.0 0.0 copy-done.6
  24.0 0.0 copy-start.5
  24.1 1.0 copy-done.5
  25.0 0.0 copy-start.7
  25.0 0.7 copy-done.7
  25.7 0.0 copy-start.8
  25.7 0.7 copy-done.8
  26.3 0.0 copy-start.9
  26.3 0.7 copy-done.9
  27.0 12.8 %chain.1 = (bf16[1,30,40,128]{3,2,1,0:T(8,128)(2,1)}, bf16[3584,128]{1,0:T(8,128)(2,1)S(1)}, bf16[3584,128]{1,0:T(8,128)(2,1)S(1)}) custom-call(bf16[2,30,40,128]{3,2,1,0:T(8,128)(2,1)S(1)} %copy-done, bf16[1,30,40,128]{3,2,1,0:T(8,128)(2,1)S(1)} %copy-done.4, bf16[2,30,40,128]{3,2,1,0:T(8,128)(2,1)S(1)} %copy-done.1, ...), custom_call_target="tpu_custom_call" | custom-call | tf_op jit(solution)/shard_map/chain/pallas_call | solution.py:255
  39.8 0.1 collective-permute-start.4
  39.9 2.5 %collective-permute-done.4 = bf16[3584,128]{1,0:T(8,128)(2,1)S(1)} collective-permute-done((bf16[3584,128]{1,0:T(8,128)(2,1)S(1)}, bf16[3584,128]{1,0:T(8,128)(2,1)S(1)}, u32[]{:S(2)}, u32[]{:S(2)}) %collective-permute-start.4) | collective-permute-done | bytes 917536 | tf_op jit(solution)/shard_map/ppermute | solution.py:282
  42.4 0.2 add_convert_fusion
  42.6 29.3 %all_to_all.10 = bf16[64,56,128]{2,1,0:T(8,128)(2,1)S(1)} all-to-all(bf16[64,56,128]{2,1,0:T(8,128)(2,1)S(1)} %bitcast.10), channel_id=1, replica_groups={{0,1,2,3,4,5,6,7,8,9,10,11,12,13,14,15,32,33,34,35,36,37,38,39,40,41,42..., dimensions={0} | all-to-all | bytes 1835008 | tf_op jit(solution)/shard_map/all_to_all | solution.py:286
  71.9 0.2 convert_reduce_fusion
  72.0 0.1 broadcast_in_dim.2
  72.2 19.5 %all_to_all.11 = bf16[64,56,128]{2,1,0:T(8,128)(2,1)S(1)} all-to-all(bf16[64,56,128]{2,1,0:T(8,128)(2,1)S(1)} %broadcast_in_dim.2), channel_id=1, replica_groups={{0,1,2,3,4,5,6,7,8,9,10,11,12,13,14,15,32,33,34,35,36,37,38,39,40,41,42..., dimensions={0} | all-to-all | bytes 1835008 | tf_op jit(solution)/shard_map/all_to_all | solution.py:286
  91.6 3.2 %collective-permute-start.5 = (bf16[3584,128]{1,0:T(8,128)(2,1)S(1)}, bf16[3584,128]{1,0:T(8,128)(2,1)S(1)}, u32[]{:S(2)}, u32[]{:S(2)}) collective-permute-start(bf16[3584,128]{1,0:T(8,128)(2,1)S(1)} %bitcast.11), channel_id=1, source_target_pairs={{0,16},{16,0},{32,48},{48,32},{64,80},{80,64},{96,112},{112,96},{1... | collective-permute-start | bytes 2752520 | tf_op jit(solution)/shard_map/ppermute | solution.py:292
  94.8 2.1 %collective-permute-done.5 = bf16[3584,128]{1,0:T(8,128)(2,1)S(1)} collective-permute-done((bf16[3584,128]{1,0:T(8,128)(2,1)S(1)}, bf16[3584,128]{1,0:T(8,128)(2,1)S(1)}, u32[]{:S(2)}, u32[]{:S(2)}) %collective-permute-start.5) | collective-permute-done | bytes 917536 | tf_op jit(solution)/shard_map/ppermute | solution.py:292
  96.9 2.0 %convert_select_fusion = (f32[3456,128]{1,0:T(8,128)}, f32[3456,128]{1,0:T(8,128)}) fusion(pred[]{:T(512)S(6)} %eq.15, bf16[3584,128]{1,0:T(8,128)(2,1)S(1)} %collective-permute-done.5, bf16[3584,128]{1,0:T(8,128)(2,1)S(1)} %bitcast.12), kind=kLoop, calls=%fused_computation | loop fusion | flops 1769472 | bytes 5308417 | tf_op jit(solution)/shard_map/jit(_where)/select_n | solution.py:297
  (3 shorter events, 0.1 us)
Async XLA Ops:
  0.6 8.0 %copy-start.4 = (bf16[1,30,40,128]{3,2,1,0:T(8,128)(2,1)S(1)}, bf16[1,30,40,128]{3,2,1,0:T(8,128)(2,1)}, u32[]{:S(2)}) copy-start(bf16[1,30,40,128]{3,2,1,0:T(8,128)(2,1)} %refs_1_.1) | copy-start | bytes 921604
  0.6 8.1 %copy-start.1 = (bf16[2,30,40,128]{3,2,1,0:T(8,128)(2,1)S(1)}, bf16[2,30,40,128]{3,2,1,0:T(8,128)(2,1)}, u32[]{:S(2)}) copy-start(bf16[2,30,40,128]{3,2,1,0:T(8,128)(2,1)} %refs_2_.1) | copy-start | bytes 1843204
  0.7 8.0 %copy-start = (bf16[2,30,40,128]{3,2,1,0:T(8,128)(2,1)S(1)}, bf16[2,30,40,128]{3,2,1,0:T(8,128)(2,1)}, u32[]{:S(2)}) copy-start(bf16[2,30,40,128]{3,2,1,0:T(8,128)(2,1)} %refs_0_.1) | copy-start | bytes 1843204
  2.7 21.3 %copy-start.2 = (bf16[3,3,3,128,128]{4,3,2,1,0:T(8,128)(2,1)S(1)}, bf16[3,3,3,128,128]{4,3,2,1,0:T(8,128)(2,1)}, u32[]{:S(2)}) copy-start(bf16[3,3,3,128,128]{4,3,2,1,0:T(8,128)(2,1)} %refs_8_.1) | copy-start | bytes 2654212
  2.7 21.3 %copy-start.3 = (bf16[3,3,3,128,128]{4,3,2,1,0:T(8,128)(2,1)S(1)}, bf16[3,3,3,128,128]{4,3,2,1,0:T(8,128)(2,1)}, u32[]{:S(2)}) copy-start(bf16[3,3,3,128,128]{4,3,2,1,0:T(8,128)(2,1)} %refs_9_.1) | copy-start | bytes 2654212
  2.7 21.3 %copy-start.6 = (f32[1,128]{1,0:T(1,128)S(1)}, f32[1,128]{1,0:T(1,128)}, u32[]{:S(2)}) copy-start(f32[1,128]{1,0:T(1,128)} %refs_10_.1) | copy-start | bytes 1540
  3.6 9.0 %collective-permute-start.1 = (bf16[6,4,40,128]{3,2,1,0:T(8,128)(2,1)}, bf16[6,4,40,128]{3,2,1,0:T(8,128)(2,1)S(1)}, u32[]{:S(2)}, u32[]{:S(2)}) collective-permute-start(bf16[6,4,40,128]{3,2,1,0:T(8,128)(2,1)} %get-tuple-element.19), channel_id=1, source_target_pairs={{16,32},{32,16},{48,64},{64,48},{80,96},{96,80},{17,33},{33,17},{4... | collective-permute-start | bytes 737288 | tf_op jit(solution)/shard_map/ppermute | solution.py:25
  8.5 4.1 %collective-permute-start = (bf16[6,4,40,128]{3,2,1,0:T(8,128)(2,1)}, bf16[6,4,40,128]{3,2,1,0:T(8,128)(2,1)}, u32[]{:S(2)}, u32[]{:S(2)}) collective-permute-start(bf16[6,4,40,128]{3,2,1,0:T(8,128)(2,1)} %get-tuple-element.20), channel_id=1, source_target_pairs={{0,16},{16,0},{32,48},{48,32},{64,80},{80,64},{96,112},{112,96},{1... | collective-permute-start | bytes 737288 | tf_op jit(solution)/shard_map/ppermute | solution.py:24
  14.6 4.4 %collective-permute-start.3 = (bf16[912,128]{1,0:T(8,128)(2,1)S(1)}, bf16[912,128]{1,0:T(8,128)(2,1)S(1)}, u32[]{:S(2)}, u32[]{:S(2)}) collective-permute-start(bf16[912,128]{1,0:T(8,128)(2,1)S(1)} %get-tuple-element.21), channel_id=1, source_target_pairs={{1,2},{2,1},{3,4},{4,3},{5,6},{6,5},{7,8},{8,7},{9,10},{10,9},{11,... | collective-permute-start | bytes 700424 | tf_op jit(solution)/shard_map/ppermute | solution.py:25
  15.3 8.8 %collective-permute-start.2 = (bf16[912,128]{1,0:T(8,128)(2,1)S(1)}, bf16[912,128]{1,0:T(8,128)(2,1)S(1)}, u32[]{:S(2)}, u32[]{:S(2)}) collective-permute-start(bf16[912,128]{1,0:T(8,128)(2,1)S(1)} %get-tuple-element.22), channel_id=1, source_target_pairs={{0,1},{1,0},{2,3},{3,2},{4,5},{5,4},{6,7},{7,6},{8,9},{9,8},{10,11... | collective-permute-start | bytes 700424 | tf_op jit(solution)/shard_map/ppermute | solution.py:24
  24.0 1.0 copy-start.5
  25.0 0.7 copy-start.7
  25.7 0.7 copy-start.8
  26.3 0.7 copy-start.9
  39.8 2.6 %collective-permute-start.4 = (bf16[3584,128]{1,0:T(8,128)(2,1)S(1)}, bf16[3584,128]{1,0:T(8,128)(2,1)S(1)}, u32[]{:S(2)}, u32[]{:S(2)}) collective-permute-start(bf16[3584,128]{1,0:T(8,128)(2,1)S(1)} %get-tuple-element.8), channel_id=1, source_target_pairs={{0,16},{16,0},{32,48},{48,32},{64,80},{80,64},{96,112},{112,96},{1... | collective-permute-start | bytes 2752520 | tf_op jit(solution)/shard_map/ppermute | solution.py:282
  91.6 5.3 %collective-permute-start.5 = (bf16[3584,128]{1,0:T(8,128)(2,1)S(1)}, bf16[3584,128]{1,0:T(8,128)(2,1)S(1)}, u32[]{:S(2)}, u32[]{:S(2)}) collective-permute-start(bf16[3584,128]{1,0:T(8,128)(2,1)S(1)} %bitcast.11), channel_id=1, source_target_pairs={{0,16},{16,0},{32,48},{48,32},{64,80},{80,64},{96,112},{112,96},{1... | collective-permute-start | bytes 2752520 | tf_op jit(solution)/shard_map/ppermute | solution.py:292

commit v2 on v1

--- a/solution.py
+++ b/solution.py
@@ -18,12 +18,9 @@
     return first, second
 
 
-def trade(axis, head, tail):
-    odd = lax.axis_index(axis) % 2 == 1
+def trade(axis, near, far):
     first, second = swaps(axis)
-    near = lax.ppermute(jnp.where(odd, head, tail), axis, first)
-    far = lax.ppermute(jnp.where(odd, tail, head), axis, second)
-    return near, far
+    return lax.ppermute(near, axis, first), lax.ppermute(far, axis, second)
 
 
 def slope(value):
@@ -33,7 +30,7 @@
 
 def chain_kernel(
     rows, cols, cache_in, frames_in, cache_mid, cot, row_near, row_far, col_near, col_far,
-    w_one, w_two, sc_one, sh_one, sc_two, sh_two,
+    corner_near, corner_far, ahead_one, ahead_two, back_one, back_two, affine,
     gin, keep, send, field, slope_one, a_one, d_two, d_one, moved, grads, sems,
 ):
     full, lanes = cols + 2 * RIM, field.shape[-1]
@@ -45,39 +42,39 @@
     def pick(odd, one, other):
         return jnp.where(odd, one.astype(F32), other.astype(F32))
 
-    def assemble(frame, top, block, at):
-        count, high = block.shape[:2]
-        size = count * high * RIM
-        near, far = col_near[at : at + size], col_far[at : at + size]
-        left = pick(odd_col, near, far).reshape(-1, 2 * RIM, lanes)
-        right = pick(odd_col, far, near).reshape(-1, 2 * RIM, lanes)
-        lower = lax.broadcasted_iota(jnp.int32, left.shape, 1) < RIM
-        rim = jnp.stack(
-            [
-                jnp.where(lower, right, pltpu.roll(left, RIM, 1)),
-                jnp.where(lower, pltpu.roll(right, RIM, 1), left),
-            ],
-            axis=1,
-        ).reshape(count, high, 2 * RIM, lanes)
-        field[frame : frame + count, top : top + high] = jnp.concatenate(
-            [block, rim], axis=2
-        ).astype(BF)
-
-    own_strip, corner = rows * RIM, RIM * RIM
-    for frame, source in ((0, cache_in), (2, frames_in), (3, cache_mid), (5, cot)):
-        assemble(frame, RIM, source[...].astype(F32), frame * own_strip)
-    near_at, far_at = 6 * own_strip, 6 * (own_strip + corner)
-    near_block, far_block = row_near[...].astype(F32), row_far[...].astype(F32)
+    def assemble(top, blocks, near, far):
+        high = blocks[0].shape[0]
+        left = pick(odd_col, near, far).reshape(high, 3, 2 * RIM, lanes)
+        right = pick(odd_col, far, near).reshape(high, 3, 2 * RIM, lanes)
+        lower = lax.broadcasted_iota(jnp.int32, (high, 2 * RIM, lanes), 1) < RIM
+        for frame, block in enumerate(blocks):
+            one, other = right[:, frame // 2], left[:, frame // 2]
+            if frame % 2 == 0:
+                rim = jnp.where(lower, one, pltpu.roll(other, RIM, 1))
+            else:
+                rim = jnp.where(lower, pltpu.roll(one, RIM, 1), other)
+            field[frame, top : top + high] = jnp.concatenate([block, rim], axis=1).astype(BF)
+
+    sources = (
+        (cache_in, 0), (cache_in, 1), (frames_in, 0), (cache_mid, 0), (cache_mid, 1), (cot, 0)
+    )
+    assemble(RIM, [ref[i].astype(F32) for ref, i in sources], col_near[...], col_far[...])
+
+    def assemble_rim(top, block, corners):
+        half = corners.shape[0] // 2
+        assemble(
+            top, [block[i].astype(F32) for i in range(6)], corners[:half], corners[half:]
+        )
 
     @pl.when(odd_row)
     def _():
-        assemble(0, 0, near_block, near_at)
-        assemble(0, RIM + rows, far_block, far_at)
+        assemble_rim(0, row_near, corner_near)
+        assemble_rim(RIM + rows, row_far, corner_far)
 
     @pl.when(jnp.logical_not(odd_row))
     def _():
-        assemble(0, 0, far_block, far_at)
-        assemble(0, RIM + rows, near_block, near_at)
+        assemble_rim(0, row_far, corner_far)
+        assemble_rim(RIM + rows, row_near, corner_near)
 
     image_rows, image_cols = rows * lax.axis_size("ha"), cols * lax.axis_size("wa")
     col = lax.broadcasted_iota(jnp.int32, (1, full, lanes), 1)
@@ -96,15 +93,7 @@
         lhs = jnp.concatenate(
             [piece(a, start - 1 + b, count) for a in range(3) for b in range(3)], axis=1
         )
-        rhs = jnp.concatenate(
-            [
-                jnp.concatenate([weight[a, b, c] for c in range(3)], axis=1)
-                for a in range(3)
-                for b in range(3)
-            ],
-            axis=0,
-        )
-        out = jnp.dot(lhs, rhs, preferred_element_type=F32).reshape(count, full, 3 * lanes)
+        out = jnp.dot(lhs, weight[...], preferred_element_type=F32).reshape(count, full, 3 * lanes)
         return (
             roll(out[..., :lanes], 1)
             + out[..., lanes : 2 * lanes]
@@ -113,12 +102,8 @@
 
     def backward(piece, weight, start, count):
         lhs = jnp.concatenate([piece(start + 1 - b, count) for b in range(3)], axis=1)
-        rhs = jnp.concatenate(
-            [jnp.concatenate([weight[2, b, c] for b in range(3)], axis=1) for c in range(3)],
-            axis=0,
-        )
         out = lax.dot_general(
-            lhs, rhs, (((1,), (1,)), ((), ())), preferred_element_type=F32
+            lhs, weight[...], (((1,), (1,)), ((), ())), preferred_element_type=F32
         ).reshape(count, full, 3 * lanes)
         return (
             roll(out[..., :lanes], -1)
@@ -157,15 +142,14 @@
     if grads.shape[1] > used:
         grads[:, used:, :] = jnp.zeros((2, grads.shape[1] - used, lanes), BF)
 
-    gain_one = (1.0 + sc_one[...]).reshape(1, 1, lanes)
-    gain_two = (1.0 + sc_two[...]).reshape(1, 1, lanes)
-    bias_one = sh_one[...].reshape(1, 1, lanes)
-    bias_two = sh_two[...].reshape(1, 1, lanes)
+    gain_one, bias_one, gain_two, bias_two = (
+        affine[i : i + 1, :].reshape(1, 1, lanes) for i in range(4)
+    )
     step = (tall - 2) // 3
     for start in range(1, tall - 1, step):
         count = min(step, tall - 1 - start)
         m_one = (
-            forward(lambda a, r, n: flat(field[a, r : r + n]), w_one, start, count) * gain_one
+            forward(lambda a, r, n: flat(field[a, r : r + n]), ahead_one, start, count) * gain_one
             + bias_one
         )
         sig = jax.nn.sigmoid(m_one)
@@ -181,7 +165,7 @@
     step = (tall - 4) // 2
     for start in range(2, tall - 2, step):
         count = min(step, tall - 2 - start)
-        m_two = forward(mid, w_two, start, count) * gain_two + bias_two
+        m_two = forward(mid, ahead_two, start, count) * gain_two + bias_two
         value = field[5, start : start + count].astype(F32) * slope(m_two) * gain_two
         d_two[start : start + count] = value.astype(BF)
         low_at, high_at = max(start, RIM), min(start + count, RIM + rows)
@@ -193,7 +177,7 @@
     for start in range(3, tall - 3, step):
         count = min(step, tall - 3 - start)
         value = (
-            backward(lambda r, n: flat(d_two[r : r + n]), w_two, start, count)
+            backward(lambda r, n: flat(d_two[r : r + n]), back_two, start, count)
             * slope_one[start : start + count]
         )
         d_one[start : start + count] = value.astype(BF)
@@ -211,11 +195,56 @@
     step = rows // 2
     for start in range(RIM, RIM + rows, step):
         count = min(step, RIM + rows - start)
-        value = backward(lambda r, n: flat(d_one[r : r + n]), w_one, start, count)
+        value = backward(lambda r, n: flat(d_one[r : r + n]), back_one, start, count)
         gin[0, start - RIM : start - RIM + count] = value[:, :cols].astype(BF)
 
     for copy in out_copies:
         copy.wait()
+
+
+def pack_kernel(rows, cols, cache_in, frames_in, cache_mid, cot, row_near, row_far, col_near, col_far):
+    odd_row, odd_col = lax.axis_index("ha") % 2 == 1, lax.axis_index("wa") % 2 == 1
+    sources = (
+        (cache_in, 0), (cache_in, 1), (frames_in, 0), (cache_mid, 0), (cache_mid, 1), (cot, 0)
+    )
+    last = rows - RIM
+    near_at, far_at = jnp.where(odd_row, 0, last), jnp.where(odd_row, last, 0)
+    for frame, (ref, i) in enumerate(sources):
+        row_near[frame] = ref[i, pl.ds(near_at, RIM)]
+        row_far[frame] = ref[i, pl.ds(far_at, RIM)]
+    lanes = col_near.shape[-1]
+    lower = lax.broadcasted_iota(jnp.int32, (rows, 2 * RIM, lanes), 1) < RIM
+
+    def edges(frame):
+        ref, i = sources[frame]
+        value = ref[i].astype(F32)
+        return value[:, : 2 * RIM], pltpu.roll(value[:, cols - 2 * RIM :], RIM, 1)
+
+    near, far = [], []
+    for pair in range(3):
+        (head, tail), (head_b, tail_b) = edges(2 * pair), edges(2 * pair + 1)
+        heads = jnp.where(lower, head, pltpu.roll(head_b, RIM, 1))
+        tails = jnp.where(lower, tail, pltpu.roll(tail_b, RIM, 1))
+        near.append(jnp.where(odd_col, heads, tails))
+        far.append(jnp.where(odd_col, tails, heads))
+    col_near[...] = jnp.stack(near, axis=1).reshape(-1, lanes).astype(BF)
+    col_far[...] = jnp.stack(far, axis=1).reshape(-1, lanes).astype(BF)
+
+
+def ready_kernel(w_one, w_two, sc_one, sh_one, sc_two, sh_two, ahead_one, ahead_two, back_one, back_two, affine):
+    lanes = affine.shape[-1]
+    for weight, ahead, back in ((w_one, ahead_one, back_one), (w_two, ahead_two, back_two)):
+        for a in range(3):
+            for b in range(3):
+                for c in range(3):
+                    at = (a * 3 + b) * lanes
+                    ahead[at : at + lanes, c * lanes : (c + 1) * lanes] = weight[a, b, c]
+        for b in range(3):
+            for c in range(3):
+                back[c * lanes : (c + 1) * lanes, b * lanes : (b + 1) * lanes] = weight[2, b, c]
+    affine[...] = jnp.concatenate(
+        [1.0 + sc_one[...], sh_one[...], 1.0 + sc_two[...], sh_two[...]] * 2, axis=0
+    )
 
 
 def per_device(
@@ -225,29 +254,49 @@
     _, rows, cols, chans = frames_in.shape
     devices = lax.axis_size("ha") * lax.axis_size("wa")
     factor = 1.0 / (rows * cols * devices) ** 0.5
-    fields = [cache_in, frames_in, cache_mid, cotangent]
-
-    def edges(cut):
-        return jnp.concatenate([cut(field) for field in fields], axis=0)
-
-    row_near, row_far = trade(
-        "ha", edges(lambda v: v[:, :RIM]), edges(lambda v: v[:, rows - RIM :])
-    )
-
-    def strip(cut):
-        pieces = [edges(cut), cut(row_near), cut(row_far)]
-        return jnp.concatenate([piece.reshape(-1, chans) for piece in pieces], axis=0)
-
-    col_near, col_far = trade(
-        "wa", strip(lambda v: v[:, :, :RIM]), strip(lambda v: v[:, :, cols - RIM :])
+    inner = pl.BlockSpec(memory_space=pltpu.VMEM)
+    anywhere = pl.BlockSpec(memory_space=pl.ANY)
+
+    def pack(*refs):
+        pack_kernel(rows, cols, *refs)
+
+    rim_rows = jax.ShapeDtypeStruct((6, RIM, cols, chans), BF)
+    rim_cols = jax.ShapeDtypeStruct((6 * rows * RIM, chans), BF)
+    row_near, row_far, col_near, col_far = pl.pallas_call(
+        pack,
+        out_shape=(rim_rows, rim_rows, rim_cols, rim_cols),
+        in_specs=[inner] * 4,
+        out_specs=(inner,) * 4,
+        compiler_params=pltpu.CompilerParams(vmem_limit_bytes=16 * 1024 * 1024),
+        name="pack",
+    )(cache_in, frames_in, cache_mid, cotangent)
+    ahead = jax.ShapeDtypeStruct((9 * chans, 3 * chans), BF)
+    back = jax.ShapeDtypeStruct((3 * chans, 3 * chans), BF)
+    ready = pl.pallas_call(
+        ready_kernel,
+        out_shape=(ahead, ahead, back, back, jax.ShapeDtypeStruct((8, chans), F32)),
+        in_specs=[inner] * 6,
+        out_specs=(inner,) * 5,
+        cost_estimate=pl.CostEstimate(
+            flops=2 * 10**9, bytes_accessed=8 * 10**6, transcendentals=0
+        ),
+        compiler_params=pltpu.CompilerParams(vmem_limit_bytes=16 * 1024 * 1024),
+        name="ready",
+    )(w_first, w_second, scale_first, shift_first, scale_second, shift_second)
+    row_near, row_far = trade("ha", row_near, row_far)
+    col_near, col_far = trade("wa", col_near, col_far)
+    size = 6 * RIM * RIM
+    head = jnp.concatenate([col_near[:size], col_far[:size]], axis=0)
+    tail = jnp.concatenate([col_near[-size:], col_far[-size:]], axis=0)
+    odd = lax.axis_index("ha") % 2 == 1
+    corner_near, corner_far = trade(
+        "ha", jnp.where(odd, head, tail), jnp.where(odd, tail, head)
     )
 
     full, tall = cols + 2 * RIM, rows + 2 * RIM
     chips = devices // 2
     total = 27 * chans
     share = -(-total // (8 * chips)) * 8
-    anywhere = pl.BlockSpec(memory_space=pl.ANY)
-    inner = pl.BlockSpec(memory_space=pltpu.VMEM)
 
     def body(*refs):
         chain_kernel(rows, cols, *refs)
@@ -259,7 +308,7 @@
             jax.ShapeDtypeStruct((share * chips, chans), BF),
             jax.ShapeDtypeStruct((share * chips, chans), BF),
         ),
-        in_specs=[inner] * 14,
+        in_specs=[inner] * 15,
         out_specs=(inner, anywhere, anywhere),
         scratch_shapes=[
             pltpu.VMEM((6, tall, full, chans), BF),
@@ -275,7 +324,7 @@
         name="chain",
     )(
         cache_in, frames_in, cache_mid, cotangent, row_near, row_far, col_near, col_far,
-        w_first, w_second, scale_first, shift_first, scale_second, shift_second,
+        corner_near, corner_far, *ready,
     )
 
     pairs, _ = swaps("ha")

time: 99.4 us -> 92 us (0.926)
  waiting for transfers between devices: 11.5 us -> 5.76 us
  other arithmetic: 5.41 us -> 2.45 us
  local copies, waits for them, and re-layouts: 6.99 us -> 4.25 us
  blocking collectives: 48.7 us -> 51.1 us
  starting transfers between devices: 12.7 us -> 14.7 us
    ppermute x4 -> x6, waiting for transfers between devices: 6.9 us -> 1.2 us  [trade(): return (lax.ppermute(near, axis, first), lax.ppermute(far, axis, second))]
    slice x8 -> x2, local copies, waits for them, and re-layouts: 3.91 us -> 0.01 us  [per_device(): head = jnp.concatenate([col_near[:size], col_far[:size]], axis=0)]
    all_to_all x2, blocking collectives: 48.7 us -> 51.1 us  [spread_out(): lax.all_to_all(value.reshape(chips, share, chans), BOTH, 0, 0, axis_index...]
    ppermute x4 -> x6, starting transfers between devices: 9.42 us -> 11.4 us  [trade(): return (lax.ppermute(near, axis, first), lax.ppermute(far, axis, second))]
    select_n x2 -> x1, other arithmetic: 1.96 us -> 0.02 us  [per_device(): jnp.where(odd, tail, head)]
    unnamed x20 -> x28, local copies, waits for them, and re-layouts: 2.96 us -> 4.12 us
    concatenate x1 -> x0, other arithmetic: 1.03 us -> none  [edges(): return jnp.concatenate([cut(field) for field in fields], axis=0)]
    pallas_call x1, Pallas kernels: 12.8 us -> 11.8 us  [per_device(): pl.pallas_call(body, out_shape=(jax.ShapeDtypeStruct((1, rows, cols, chan...]
  transfers between devices with their start and end apart: 6 -> 8, of which waited for: 4 -> 3; matrix products, arithmetic and copies ran while one was open for 2% -> 0% of each run, Pallas kernels for 0% -> 0%
where the time goes in v2:
time: 92 us; the launch traced here: 91.6 us
  blocking collectives  51.1 us (56%)
  starting transfers between devices  14.7 us (16%)
  Pallas kernels  12.3 us (13%)
  waiting for transfers between devices  5.76 us (6%)
  local copies, waits for them, and re-layouts  4.25 us (5%)
  other arithmetic  2.45 us (3%)
    all_to_all x2, blocking collectives, spread_out(): lax.all_to_all(value.reshape(chips, share, chans), BOTH, 0, 0, axis_index...  51.1 us
    pallas_call x1, Pallas kernels, per_device(): pl.pallas_call(body, out_shape=(jax.ShapeDtypeStruct((1, rows, cols, chan...  11.8 us
    ppermute x6, starting transfers between devices, trade(): return (lax.ppermute(near, axis, first), lax.ppermute(far, axis, second))  11.4 us
    unnamed x28, local copies, waits for them, and re-layouts  4.12 us
    ppermute x1, starting transfers between devices, per_device(): other = lax.ppermute(one, 'ha', pairs)  3.19 us
    ppermute x1, waiting for transfers between devices, per_device(): lax.ppermute(send, 'ha', pairs).astype(F32)  2.46 us
    ppermute x1, waiting for transfers between devices, per_device(): other = lax.ppermute(one, 'ha', pairs)  2.1 us
    select_n x1, other arithmetic, per_device(): grad_second = jnp.where(even, other, one).reshape(shape)  2.02 us
  transfers between devices with their start and end apart: 8, of which 3 were waited for; matrix products, arithmetic and copies ran while one was open for 0% of the time, Pallas kernels for 0%

profile of v2, /device:TPU:1, one launch (start us, length us, event | category | flops | bytes accessed | tf_op | source)
XLA Modules:
  0.0 91.6 jit_solution(2843046747040888441)
XLA Ops:
  0.6 0.0 copy-start
  0.6 1.1 %copy-done = bf16[2,30,40,128]{3,2,1,0:T(8,128)(2,1)S(1)} copy-done((bf16[2,30,40,128]{3,2,1,0:T(8,128)(2,1)S(1)}, bf16[2,30,40,128]{3,2,1,0:T(8,128)(2,1)}, u32[]{:S(2)}) %copy-start) | copy-done | bytes 614424
  1.7 0.0 copy-start.2
  1.7 1.1 %copy-done.2 = bf16[2,30,40,128]{3,2,1,0:T(8,128)(2,1)S(1)} copy-done((bf16[2,30,40,128]{3,2,1,0:T(8,128)(2,1)S(1)}, bf16[2,30,40,128]{3,2,1,0:T(8,128)(2,1)}, u32[]{:S(2)}) %copy-start.2) | copy-done | bytes 614424
  2.8 0.0 copy-start.4
  2.8 1.0 %copy-done.4 = bf16[1,30,40,128]{3,2,1,0:T(8,128)(2,1)S(1)} copy-done((bf16[1,30,40,128]{3,2,1,0:T(8,128)(2,1)S(1)}, bf16[1,30,40,128]{3,2,1,0:T(8,128)(2,1)}, u32[]{:S(2)}) %copy-start.4) | copy-done | bytes 307224
  3.7 0.0 copy-start.6
  3.8 1.0 %copy-done.6 = bf16[1,30,40,128]{3,2,1,0:T(8,128)(2,1)S(1)} copy-done((bf16[1,30,40,128]{3,2,1,0:T(8,128)(2,1)S(1)}, bf16[1,30,40,128]{3,2,1,0:T(8,128)(2,1)}, u32[]{:S(2)}) %copy-start.6) | copy-done | bytes 307224
  4.7 0.0 copy-start.8
  4.7 0.0 copy-start.9
  4.7 0.0 copy-start.10
  4.7 0.0 copy-start.11
  4.7 0.0 copy-start.12
  4.7 0.0 copy-start.13
  4.7 0.2 pack.1
  4.9 2.1 %collective-permute-start.2 = (bf16[720,128]{1,0:T(8,128)(2,1)S(1)}, bf16[720,128]{1,0:T(8,128)(2,1)S(1)}, u32[]{:S(2)}, u32[]{:S(2)}) collective-permute-start(bf16[720,128]{1,0:T(8,128)(2,1)S(1)} %get-tuple-element.17), channel_id=1, source_target_pairs={{0,1},{1,0},{2,3},{3,2},{4,5},{5,4},{6,7},{7,6},{8,9},{9,8},{10,11... | collective-permute-start | bytes 552968 | tf_op jit(solution)/shard_map/ppermute | solution.py:23
  7.0 0.7 collective-permute-start.3
  7.7 1.0 %collective-permute-start = (bf16[6,4,40,128]{3,2,1,0:T(8,128)(2,1)S(1)}, bf16[6,4,40,128]{3,2,1,0:T(8,128)(2,1)S(1)}, u32[]{:S(2)}, u32[]{:S(2)}) collective-permute-start(bf16[6,4,40,128]{3,2,1,0:T(8,128)(2,1)S(1)} %get-tuple-element.15), channel_id=1, source_target_pairs={{0,16},{16,0},{32,48},{48,32},{64,80},{80,64},{96,112},{112,96},{1... | collective-permute-start | bytes 737288 | tf_op jit(solution)/shard_map/ppermute | solution.py:23
  8.7 3.4 %collective-permute-start.1 = (bf16[6,4,40,128]{3,2,1,0:T(8,128)(2,1)S(1)}, bf16[6,4,40,128]{3,2,1,0:T(8,128)(2,1)S(1)}, u32[]{:S(2)}, u32[]{:S(2)}) collective-permute-start(bf16[6,4,40,128]{3,2,1,0:T(8,128)(2,1)S(1)} %get-tuple-element.16), channel_id=1, source_target_pairs={{16,32},{32,16},{48,64},{64,48},{80,96},{96,80},{17,33},{33,17},{4... | collective-permute-start | bytes 737288 | tf_op jit(solution)/shard_map/ppermute | solution.py:23
  12.2 0.0 collective-permute-done.2.refs_6_
  12.2 0.0 collective-permute-done.3.refs_7_
  12.3 4.1 %collective-permute-start.5 = (bf16[192,128]{1,0:T(8,128)(2,1)S(1)}, bf16[192,128]{1,0:T(8,128)(2,1)S(1)}, u32[]{:S(2)}, u32[]{:S(2)}) collective-permute-start(bf16[192,128]{1,0:T(8,128)(2,1)S(1)} %get-tuple-element.33), channel_id=1, source_target_pairs={{16,32},{32,16},{48,64},{64,48},{80,96},{96,80},{17,33},{33,17},{4... | collective-permute-start | bytes 147464 | tf_op jit(solution)/shard_map/ppermute | solution.py:23
  16.4 0.0 copy-start.1
  16.4 0.0 copy-start.3
  16.4 0.0 copy-start.5
  16.4 0.0 copy-start.7
  16.4 0.1 collective-permute-start.4
  16.5 0.0 copy-done.8
  16.5 0.0 copy-done.9
  16.5 0.0 copy-done.10
  16.6 0.0 copy-done.11
  16.6 0.0 copy-done.12
  16.6 0.0 copy-done.13
  16.6 0.4 ready.1
  16.9 1.2 %collective-permute-done.5.refs_9_ = bf16[192,128]{1,0:T(8,128)(2,1)S(1)} collective-permute-done((bf16[192,128]{1,0:T(8,128)(2,1)S(1)}, bf16[192,128]{1,0:T(8,128)(2,1)S(1)}, u32[]{:S(2)}, u32[]{:S(2)}) %collective-permute-start.5) | collective-permute-done | bytes 49184 | tf_op jit(solution)/shard_map/ppermute | solution.py:23
  18.1 0.0 collective-permute-done.4.refs_8_
  18.1 0.0 collective-permute-done.refs_4_
  18.1 0.0 collective-permute-done.1.refs_5_
  18.2 0.0 copy-done.1
  18.2 0.0 copy-done.3
  18.2 0.0 copy-done.5
  18.2 0.0 copy-done.7
  18.2 11.8 %chain.1 = (bf16[1,30,40,128]{3,2,1,0:T(8,128)(2,1)}, bf16[3584,128]{1,0:T(8,128)(2,1)S(1)}, bf16[3584,128]{1,0:T(8,128)(2,1)S(1)}) custom-call(bf16[2,30,40,128]{3,2,1,0:T(8,128)(2,1)S(1)} %copy-done.1, bf16[1,30,40,128]{3,2,1,0:T(8,128)(2,1)S(1)} %copy-done.5, bf16[2,30,40,128]{3,2,1,0:T(8,128)(2,1)S(1)} %copy-done.3, ...), custom_call_target="tpu_custom_call" | custom-call | tf_op jit(solution)/shard_map/chain/pallas_call | solution.py:304
  30.0 0.1 collective-permute-start.6
  30.1 2.5 %collective-permute-done.6 = bf16[3584,128]{1,0:T(8,128)(2,1)S(1)} collective-permute-done((bf16[3584,128]{1,0:T(8,128)(2,1)S(1)}, bf16[3584,128]{1,0:T(8,128)(2,1)S(1)}, u32[]{:S(2)}, u32[]{:S(2)}) %collective-permute-start.6) | collective-permute-done | bytes 917536 | tf_op jit(solution)/shard_map/ppermute | solution.py:331
  32.6 0.2 add_convert_fusion
  32.8 31.7 %all_to_all.10 = bf16[64,56,128]{2,1,0:T(8,128)(2,1)S(1)} all-to-all(bf16[64,56,128]{2,1,0:T(8,128)(2,1)S(1)} %bitcast.4), channel_id=1, replica_groups={{0,1,2,3,4,5,6,7,8,9,10,11,12,13,14,15,32,33,34,35,36,37,38,39,40,41,42..., dimensions={0} | all-to-all | bytes 1835008 | tf_op jit(solution)/shard_map/all_to_all | solution.py:335
  64.5 0.2 convert_reduce_fusion
  64.7 0.1 broadcast_in_dim.2
  64.8 19.5 %all_to_all.11 = bf16[64,56,128]{2,1,0:T(8,128)(2,1)S(1)} all-to-all(bf16[64,56,128]{2,1,0:T(8,128)(2,1)S(1)} %broadcast_in_dim.2), channel_id=1, replica_groups={{0,1,2,3,4,5,6,7,8,9,10,11,12,13,14,15,32,33,34,35,36,37,38,39,40,41,42..., dimensions={0} | all-to-all | bytes 1835008 | tf_op jit(solution)/shard_map/all_to_all | solution.py:335
  84.2 3.2 %collective-permute-start.7 = (bf16[3584,128]{1,0:T(8,128)(2,1)S(1)}, bf16[3584,128]{1,0:T(8,128)(2,1)S(1)}, u32[]{:S(2)}, u32[]{:S(2)}) collective-permute-start(bf16[3584,128]{1,0:T(8,128)(2,1)S(1)} %bitcast.5), channel_id=1, source_target_pairs={{0,16},{16,0},{32,48},{48,32},{64,80},{80,64},{96,112},{112,96},{1... | collective-permute-start | bytes 2752520 | tf_op jit(solution)/shard_map/ppermute | solution.py:341
  87.4 2.1 %collective-permute-done.7 = bf16[3584,128]{1,0:T(8,128)(2,1)S(1)} collective-permute-done((bf16[3584,128]{1,0:T(8,128)(2,1)S(1)}, bf16[3584,128]{1,0:T(8,128)(2,1)S(1)}, u32[]{:S(2)}, u32[]{:S(2)}) %collective-permute-start.7) | collective-permute-done | bytes 917536 | tf_op jit(solution)/shard_map/ppermute | solution.py:341
  89.5 2.0 %convert_select_fusion = (f32[3456,128]{1,0:T(8,128)}, f32[3456,128]{1,0:T(8,128)}) fusion(pred[]{:T(512)S(6)} %eq.10, bf16[3584,128]{1,0:T(8,128)(2,1)S(1)} %collective-permute-done.7, bf16[3584,128]{1,0:T(8,128)(2,1)S(1)} %bitcast.6), kind=kLoop, calls=%fused_computation | loop fusion | flops 1769472 | bytes 5308417 | tf_op jit(solution)/shard_map/jit(_where)/select_n | solution.py:346
  (4 shorter events, 0.0 us)
Async XLA Ops:
  0.6 1.1 %copy-start = (bf16[2,30,40,128]{3,2,1,0:T(8,128)(2,1)S(1)}, bf16[2,30,40,128]{3,2,1,0:T(8,128)(2,1)}, u32[]{:S(2)}) copy-start(bf16[2,30,40,128]{3,2,1,0:T(8,128)(2,1)} %refs_0_.3) | copy-start | bytes 1843204
  1.7 1.1 %copy-start.2 = (bf16[2,30,40,128]{3,2,1,0:T(8,128)(2,1)S(1)}, bf16[2,30,40,128]{3,2,1,0:T(8,128)(2,1)}, u32[]{:S(2)}) copy-start(bf16[2,30,40,128]{3,2,1,0:T(8,128)(2,1)} %refs_2_.3) | copy-start | bytes 1843204
  2.8 1.0 %copy-start.4 = (bf16[1,30,40,128]{3,2,1,0:T(8,128)(2,1)S(1)}, bf16[1,30,40,128]{3,2,1,0:T(8,128)(2,1)}, u32[]{:S(2)}) copy-start(bf16[1,30,40,128]{3,2,1,0:T(8,128)(2,1)} %refs_1_.3) | copy-start | bytes 921604
  3.7 1.0 %copy-start.6 = (bf16[1,30,40,128]{3,2,1,0:T(8,128)(2,1)S(1)}, bf16[1,30,40,128]{3,2,1,0:T(8,128)(2,1)}, u32[]{:S(2)}) copy-start(bf16[1,30,40,128]{3,2,1,0:T(8,128)(2,1)} %refs_3_.3) | copy-start | bytes 921604
  4.7 11.8 %copy-start.8 = (bf16[3,3,3,128,128]{4,3,2,1,0:T(8,128)(2,1)S(1)}, bf16[3,3,3,128,128]{4,3,2,1,0:T(8,128)(2,1)}, u32[]{:S(2)}) copy-start(bf16[3,3,3,128,128]{4,3,2,1,0:T(8,128)(2,1)} %w_one.1) | copy-start | bytes 2654212
  4.7 11.8 %copy-start.9 = (bf16[3,3,3,128,128]{4,3,2,1,0:T(8,128)(2,1)S(1)}, bf16[3,3,3,128,128]{4,3,2,1,0:T(8,128)(2,1)}, u32[]{:S(2)}) copy-start(bf16[3,3,3,128,128]{4,3,2,1,0:T(8,128)(2,1)} %w_two.1) | copy-start | bytes 2654212
  4.7 11.8 %copy-start.10 = (f32[1,128]{1,0:T(1,128)S(1)}, f32[1,128]{1,0:T(1,128)}, u32[]{:S(2)}) copy-start(f32[1,128]{1,0:T(1,128)} %sc_one.1) | copy-start | bytes 1540
  4.7 11.8 %copy-start.11 = (f32[1,128]{1,0:T(1,128)S(1)}, f32[1,128]{1,0:T(1,128)}, u32[]{:S(2)}) copy-start(f32[1,128]{1,0:T(1,128)} %sh_one.1) | copy-start | bytes 1540
  4.7 11.8 %copy-start.12 = (f32[1,128]{1,0:T(1,128)S(1)}, f32[1,128]{1,0:T(1,128)}, u32[]{:S(2)}) copy-start(f32[1,128]{1,0:T(1,128)} %sc_two.1) | copy-start | bytes 1540
  4.7 11.8 %copy-start.13 = (f32[1,128]{1,0:T(1,128)S(1)}, f32[1,128]{1,0:T(1,128)}, u32[]{:S(2)}) copy-start(f32[1,128]{1,0:T(1,128)} %sh_two.1) | copy-start | bytes 1540
  4.9 7.3 %collective-permute-start.2 = (bf16[720,128]{1,0:T(8,128)(2,1)S(1)}, bf16[720,128]{1,0:T(8,128)(2,1)S(1)}, u32[]{:S(2)}, u32[]{:S(2)}) collective-permute-start(bf16[720,128]{1,0:T(8,128)(2,1)S(1)} %get-tuple-element.17), channel_id=1, source_target_pairs={{0,1},{1,0},{2,3},{3,2},{4,5},{5,4},{6,7},{7,6},{8,9},{9,8},{10,11... | collective-permute-start | bytes 552968 | tf_op jit(solution)/shard_map/ppermute | solution.py:23
  7.0 5.2 %collective-permute-start.3 = (bf16[720,128]{1,0:T(8,128)(2,1)S(1)}, bf16[720,128]{1,0:T(8,128)(2,1)S(1)}, u32[]{:S(2)}, u32[]{:S(2)}) collective-permute-start(bf16[720,128]{1,0:T(8,128)(2,1)S(1)} %get-tuple-element.18), channel_id=1, source_target_pairs={{1,2},{2,1},{3,4},{4,3},{5,6},{6,5},{7,8},{8,7},{9,10},{10,9},{11,... | collective-permute-start | bytes 552968 | tf_op jit(solution)/shard_map/ppermute | solution.py:23
  7.7 10.4 %collective-permute-start = (bf16[6,4,40,128]{3,2,1,0:T(8,128)(2,1)S(1)}, bf16[6,4,40,128]{3,2,1,0:T(8,128)(2,1)S(1)}, u32[]{:S(2)}, u32[]{:S(2)}) collective-permute-start(bf16[6,4,40,128]{3,2,1,0:T(8,128)(2,1)S(1)} %get-tuple-element.15), channel_id=1, source_target_pairs={{0,16},{16,0},{32,48},{48,32},{64,80},{80,64},{96,112},{112,96},{1... | collective-permute-start | bytes 737288 | tf_op jit(solution)/shard_map/ppermute | solution.py:23
  8.7 9.4 %collective-permute-start.1 = (bf16[6,4,40,128]{3,2,1,0:T(8,128)(2,1)S(1)}, bf16[6,4,40,128]{3,2,1,0:T(8,128)(2,1)S(1)}, u32[]{:S(2)}, u32[]{:S(2)}) collective-permute-start(bf16[6,4,40,128]{3,2,1,0:T(8,128)(2,1)S(1)} %get-tuple-element.16), channel_id=1, source_target_pairs={{16,32},{32,16},{48,64},{64,48},{80,96},{96,80},{17,33},{33,17},{4... | collective-permute-start | bytes 737288 | tf_op jit(solution)/shard_map/ppermute | solution.py:23
  12.3 5.8 %collective-permute-start.5 = (bf16[192,128]{1,0:T(8,128)(2,1)S(1)}, bf16[192,128]{1,0:T(8,128)(2,1)S(1)}, u32[]{:S(2)}, u32[]{:S(2)}) collective-permute-start(bf16[192,128]{1,0:T(8,128)(2,1)S(1)} %get-tuple-element.33), channel_id=1, source_target_pairs={{16,32},{32,16},{48,64},{64,48},{80,96},{96,80},{17,33},{33,17},{4... | collective-permute-start | bytes 147464 | tf_op jit(solution)/shard_map/ppermute | solution.py:23
  16.4 1.8 %copy-start.1 = (bf16[2,30,40,128]{3,2,1,0:T(8,128)(2,1)S(1)}, bf16[2,30,40,128]{3,2,1,0:T(8,128)(2,1)}, u32[]{:S(2)}) copy-start(bf16[2,30,40,128]{3,2,1,0:T(8,128)(2,1)} %refs_0_.3) | copy-start | bytes 1843204
  16.4 1.8 %copy-start.3 = (bf16[2,30,40,128]{3,2,1,0:T(8,128)(2,1)S(1)}, bf16[2,30,40,128]{3,2,1,0:T(8,128)(2,1)}, u32[]{:S(2)}) copy-start(bf16[2,30,40,128]{3,2,1,0:T(8,128)(2,1)} %refs_2_.3) | copy-start | bytes 1843204
  16.4 1.8 %copy-start.5 = (bf16[1,30,40,128]{3,2,1,0:T(8,128)(2,1)S(1)}, bf16[1,30,40,128]{3,2,1,0:T(8,128)(2,1)}, u32[]{:S(2)}) copy-start(bf16[1,30,40,128]{3,2,1,0:T(8,128)(2,1)} %refs_1_.3) | copy-start | bytes 921604
  16.4 1.8 %copy-start.7 = (bf16[1,30,40,128]{3,2,1,0:T(8,128)(2,1)S(1)}, bf16[1,30,40,128]{3,2,1,0:T(8,128)(2,1)}, u32[]{:S(2)}) copy-start(bf16[1,30,40,128]{3,2,1,0:T(8,128)(2,1)} %refs_3_.3) | copy-start | bytes 921604
  16.4 1.7 %collective-permute-start.4 = (bf16[192,128]{1,0:T(8,128)(2,1)S(1)}, bf16[192,128]{1,0:T(8,128)(2,1)S(1)}, u32[]{:S(2)}, u32[]{:S(2)}) collective-permute-start(bf16[192,128]{1,0:T(8,128)(2,1)S(1)} %get-tuple-element.34), channel_id=1, source_target_pairs={{0,16},{16,0},{32,48},{48,32},{64,80},{80,64},{96,112},{112,96},{1... | collective-permute-start | bytes 147464 | tf_op jit(solution)/shard_map/ppermute | solution.py:23
  30.0 2.6 %collective-permute-start.6 = (bf16[3584,128]{1,0:T(8,128)(2,1)S(1)}, bf16[3584,128]{1,0:T(8,128)(2,1)S(1)}, u32[]{:S(2)}, u32[]{:S(2)}) collective-permute-start(bf16[3584,128]{1,0:T(8,128)(2,1)S(1)} %get-tuple-element.26), channel_id=1, source_target_pairs={{0,16},{16,0},{32,48},{48,32},{64,80},{80,64},{96,112},{112,96},{1... | collective-permute-start | bytes 2752520 | tf_op jit(solution)/shard_map/ppermute | solution.py:331
  84.2 5.3 %collective-permute-start.7 = (bf16[3584,128]{1,0:T(8,128)(2,1)S(1)}, bf16[3584,128]{1,0:T(8,128)(2,1)S(1)}, u32[]{:S(2)}, u32[]{:S(2)}) collective-permute-start(bf16[3584,128]{1,0:T(8,128)(2,1)S(1)} %bitcast.5), channel_id=1, source_target_pairs={{0,16},{16,0},{32,48},{48,32},{64,80},{80,64},{96,112},{112,96},{1... | collective-permute-start | bytes 2752520 | tf_op jit(solution)/shard_map/ppermute | solution.py:341
